TPU v7x, 32 devices: a whole 2x2x4 slice. The times are simulated.
32 devices in a mesh: req: 8 (over z, y), tp: 4 (over x, core).
Axes of the slice: x: 2, y: 2, z: 4, core: 2. Of those that a mesh axis runs over, the one named last changes fastest.
Arguments:
- queries: bfloat16 [4096, 8192], P('req', 'tp'), may hold values from -6 to 6
- suffix_kv: bfloat16 [2, 4096, 1024], P(None, 'req', 'tp'), may hold values from -6 to 6
- page_pool: bfloat16 [512, 2, 64, 1024], P('req', None, None, 'tp'), may hold values from -6 to 6
- prefix_pages: int32 [8, 64], P('req'), may hold values from -1 to 511, as said below
- prefix_len: int32 [8], P('req'), may hold values from 2048 to 4096, as said below
- mamba_x: bfloat16 [4096, 8192], P('req', 'tp'), may hold values from -6 to 6
- gate_z: bfloat16 [4096, 8192], P('req', 'tp'), may hold values from -6 to 6
- x_proj: bfloat16 [8192, 544], P('tp'), may hold values from -0.0625 to 0.0625
- dt_proj: bfloat16 [512, 8192], P(None, 'tp'), may hold values from -0.25 to 0.25
- dt_bias: float32 [8192], P('tp'), may hold values from -9 to -4
- decay_rate: float32 [16, 8192], P(None, 'tp'), may hold values from 1 to 8
- skip_gain: float32 [8192], P('tp'), may hold values from 0.5 to 1.5
- state_pool: bfloat16 [32, 16, 8192], P('req', None, 'tp'), may hold values from -6 to 6
- state_src: int32 [8], P('req'), may hold values from 0 to 31
Outputs:
- attn_out: bfloat16 [4096, 8192], P('req', 'tp')
- mamba_out: bfloat16 [4096, 8192], P('req', 'tp')
Inputs may be any that keep to these rules, and one draw needn't show every extreme that they name: `prefix_len`: some request has exactly 4096 cached tokens. `prefix_pages`: slot j of request r holds a page index for j < ceil(prefix_len[r] / 64) and -1 after; page p is row p % 64 of the pages kept by index p // 64 of req. Pages may repeat. Of one request's pages, at most 9 are kept by one index of req, and for every request exactly 9 are kept by some index.
All inputs are finite; a program needn't handle non-finite values.
Results may differ from a plain program's by a relative error of at most 0.012.
Values may be sent and summed in bfloat16 or wider, within the bound.
A program may use at most 192 MiB of HBM per device.

v0:
```python
import functools
import math

import jax
import jax.numpy as jnp
from jax import lax
from jax.experimental import pallas as pl
from jax.experimental.pallas import tpu as pltpu
from jax.sharding import PartitionSpec as P

HEADS = 64
KV_HEADS = 8
HEAD_DIM = 128
STATE = 16
DT_RANK = 512
MAXPG = 64
LANES = 128
KEY_BLOCK = 1024
STEP_HEADS = 2
LOG2E = 1.4426950408889634


def page_places(pages, pool_dev, cap):
    keeper = jnp.where(pages >= 0, pages // pool_dev, -1)
    index = jnp.arange(pages.shape[-1])
    earlier = (keeper[..., :, None] == keeper[..., None, :]) & (index[None, :] < index[:, None])
    rank = jnp.sum(earlier.astype(jnp.int32), axis=-1)
    return jnp.where(pages >= 0, keeper * cap + rank, -1)


def pack_asks(pages, places, pool_dev, targets):
    local = jnp.where(pages >= 0, pages % pool_dev, 0)
    hit = places[..., None, :] == targets[:, None]
    return jnp.sum(jnp.where(hit, local[..., None, :] + 1, 0), axis=-1) - 1


def gather_kernel(slots, parts, asks, pool, *rest):
    outs, sem = rest[:parts], rest[parts]

    def start(slot, carry):
        page = jnp.maximum(asks[slot], 0)
        for part in range(parts):
            pltpu.make_async_copy(
                pool.at[page, :, :, pl.ds(part * LANES, LANES)],
                outs[part].at[slot],
                sem.at[part],
            ).start()
        return carry

    lax.fori_loop(0, slots, start, 0)
    for part in range(parts):
        pltpu.make_async_copy(outs[part], outs[part], sem.at[part]).wait()


def gather_pages(page_pool, asks):
    slots = asks.shape[0]
    parts = page_pool.shape[3] // LANES
    one = jax.ShapeDtypeStruct((slots,) + page_pool.shape[1:3] + (LANES,), page_pool.dtype)
    return pl.pallas_call(
        functools.partial(gather_kernel, slots, parts),
        out_shape=(one,) * parts,
        in_specs=[
            pl.BlockSpec(memory_space=pltpu.SMEM),
            pl.BlockSpec(memory_space=pl.ANY),
        ],
        out_specs=(pl.BlockSpec(memory_space=pl.ANY),) * parts,
        scratch_shapes=[pltpu.SemaphoreType.DMA((parts,))],
        name="gather_pages",
    )(asks, page_pool)


def dot_nt(a, b):
    return lax.dot_general(a, b, (((1,), (1,)), ((), ())), preferred_element_type=jnp.float32)


def attend_kernel(places, plen_ref, q_ref, kv_ref, pages_ref, *rest):
    o_ref, k_s, v_s, sv_s, m_s, a_s, sem = rest[-7:]
    rows = q_ref.shape[0]
    page_rows = pages_ref.shape[2]
    keys = k_s.shape[0]
    slots = keys // page_rows
    scale = HEAD_DIM ** (-0.5) * LOG2E
    first = pl.program_id(0) == 0

    @pl.when(first)
    def _():
        def start(slot, carry):
            page = jnp.maximum(places[slot], 0)
            at = pl.ds(pl.multiple_of(slot * page_rows, page_rows), page_rows)
            pltpu.make_async_copy(pages_ref.at[page, 0], k_s.at[at], sem.at[0]).start()
            pltpu.make_async_copy(
                pages_ref.at[page, 1], v_s.at[at, pl.ds(0, LANES)], sem.at[1]
            ).start()
            return carry

        lax.fori_loop(0, slots, start, 0)
        v_s[:, LANES:] = jnp.ones((keys, LANES), v_s.dtype)
        sv_s[:, :LANES] = kv_ref[1]
        sv_s[:, LANES:] = jnp.ones((rows, LANES), sv_s.dtype)

    half = rows // 2
    for head in range(STEP_HEADS):
        for part in range(2):
            own = slice(part * half, (part + 1) * half)
            seen = (part + 1) * half
            q = q_ref[own, head * LANES : (head + 1) * LANES]
            s = dot_nt(q, kv_ref[0, :seen]) * scale
            row = lax.broadcasted_iota(jnp.int32, s.shape, 0) + part * half
            col = lax.broadcasted_iota(jnp.int32, s.shape, 1)
            s = jnp.where(col <= row, s, -1e30)
            m = jnp.max(s, axis=1, keepdims=True)
            p = jnp.exp2(s - m).astype(jnp.bfloat16)
            m_s[head, own] = jnp.broadcast_to(m, (half, LANES))
            a_s[head, own] = jnp.dot(p, sv_s[:seen], preferred_element_type=jnp.float32)

    @pl.when(first)
    def _():
        pltpu.make_async_copy(k_s, k_s, sem.at[0]).wait()
        pltpu.make_async_copy(v_s.at[:, pl.ds(0, LANES)], v_s.at[:, pl.ds(0, LANES)], sem.at[1]).wait()

    plen = plen_ref[0]
    last = (plen + KEY_BLOCK - 1) // KEY_BLOCK - 1

    def fold(block, masked):
        at = pl.ds(pl.multiple_of(block * KEY_BLOCK, KEY_BLOCK), KEY_BLOCK)
        k = k_s[at]
        v = v_s[at]
        if masked:
            col = lax.broadcasted_iota(jnp.int32, (1, KEY_BLOCK), 1) + block * KEY_BLOCK
            bias = jnp.where(col < plen, 0.0, -1e30)
        for head in range(STEP_HEADS):
            q = q_ref[:, head * LANES : (head + 1) * LANES]
            s = dot_nt(q, k) * scale
            if masked:
                s = s + bias
            old = m_s[head]
            new = jnp.maximum(old, jnp.max(s, axis=1, keepdims=True))
            m_s[head] = new
            fade = jnp.exp2(old - new)
            p = jnp.exp2(s - jnp.tile(new, (1, KEY_BLOCK // LANES))).astype(jnp.bfloat16)
            a_s[head] = a_s[head] * jnp.tile(fade, (1, 2)) + jnp.dot(
                p, v, preferred_element_type=jnp.float32
            )

    def visit(block, carry):
        fold(block, False)
        return carry

    lax.fori_loop(0, last, visit, 0)
    fold(last, True)
    for head in range(STEP_HEADS):
        o_ref[:, head * LANES : (head + 1) * LANES] = (
            a_s[head, :, :LANES] / a_s[head, :, LANES:]
        ).astype(o_ref.dtype)


def attend(part, places, plen, queries, suffix_kv, pages, out):
    rows, width = queries.shape
    group = HEADS // KV_HEADS
    steps = group // STEP_HEADS
    wide = STEP_HEADS * HEAD_DIM
    keys = places.shape[0] * pages.shape[2]
    in_specs = [
        pl.BlockSpec((rows, wide), lambda i, *_: (0, part * steps + i)),
        pl.BlockSpec((2, rows, HEAD_DIM), lambda i, *_: (0, 0, part)),
        pl.BlockSpec(memory_space=pl.ANY),
    ]
    args = [places, plen, queries, suffix_kv, pages]
    aliases = {}
    if out is not None:
        in_specs.append(pl.BlockSpec(memory_space=pl.ANY))
        args.append(out)
        aliases = {5: 0}
    flops = 4 * rows * group * (keys + rows) * HEAD_DIM
    return pl.pallas_call(
        attend_kernel,
        out_shape=jax.ShapeDtypeStruct((rows, width), jnp.bfloat16),
        grid_spec=pltpu.PrefetchScalarGridSpec(
            num_scalar_prefetch=2,
            grid=(steps,),
            in_specs=in_specs,
            out_specs=pl.BlockSpec((rows, wide), lambda i, *_: (0, part * steps + i)),
            scratch_shapes=[
                pltpu.VMEM((keys, HEAD_DIM), jnp.bfloat16),
                pltpu.VMEM((keys, 2 * LANES), jnp.bfloat16),
                pltpu.VMEM((rows, 2 * LANES), jnp.bfloat16),
                pltpu.VMEM((STEP_HEADS, rows, LANES), jnp.float32),
                pltpu.VMEM((STEP_HEADS, rows, 2 * LANES), jnp.float32),
                pltpu.SemaphoreType.DMA((2,)),
            ],
        ),
        input_output_aliases=aliases,
        compiler_params=pltpu.CompilerParams(vmem_limit_bytes=48 * 2**20),
        cost_estimate=pl.CostEstimate(
            flops=2 * flops, bytes_accessed=8 * 2**20, transcendentals=flops // (4 * HEAD_DIM)
        ),
        name="attend_cached",
    )(*args)


def scan_kernel(
    cols_ref, dtp_ref, bias_ref, x_ref, z_ref, rate_ref, skip_ref, h0_ref, o_ref, d_s, u_s, y_s, bc_s
):
    rows, width = x_ref.shape
    tiles = width // LANES
    packs = tiles // 8
    low = cols_ref[:, :DT_RANK].astype(jnp.float32)
    low = (low * lax.rsqrt(jnp.mean(low * low, axis=-1, keepdims=True) + 1e-06)).astype(
        jnp.bfloat16
    )
    for tile in range(tiles):
        at = slice(tile * LANES, (tile + 1) * LANES)
        if tile % 2 == 0:
            two = slice(tile * LANES, (tile + 2) * LANES)
            pair = (
                jnp.dot(low, dtp_ref[:, two], preferred_element_type=jnp.float32)
                + bias_ref[:, two]
            )
        v = pair[:, (tile % 2) * LANES : (tile % 2 + 1) * LANES]
        step = jnp.maximum(v, 0.0) + jnp.log1p(jnp.exp(-jnp.abs(v)))
        spread = pl.ds(tile, rows, stride=tiles)
        d_s[spread, :] = step
        u_s[spread, :] = step * x_ref[:, at].astype(jnp.float32)
    maps = cols_ref[:, DT_RANK:].astype(jnp.float32)
    for entry in range(2 * STATE):
        bc_s[entry] = jnp.broadcast_to(maps[:, entry : entry + 1], (rows, LANES))

    def advance(group, states):
        states = list(states)
        for inner in range(8):
            token = group * 8 + inner
            base = pl.multiple_of(token * tiles, tiles)
            d = [d_s[pl.ds(base + 8 * p, 8), :] for p in range(packs)]
            u = [u_s[pl.ds(base + 8 * p, 8), :] for p in range(packs)]
            y = [None] * packs
            for n in range(STATE):
                b = bc_s[n, pl.ds(token, 1), :]
                c = bc_s[STATE + n, pl.ds(token, 1), :]
                for p in range(packs):
                    k = n * packs + p
                    fade = jnp.exp2(d[p] * rate_ref[n, 8 * p : 8 * p + 8, :])
                    states[k] = fade * states[k] + u[p] * b
                    term = c * states[k]
                    y[p] = term if y[p] is None else y[p] + term
            for p in range(packs):
                y_s[pl.ds(base + 8 * p, 8), :] = y[p]
        return tuple(states)

    start = tuple(
        h0_ref[n, 8 * p : 8 * p + 8, :] for n in range(STATE) for p in range(packs)
    )
    lax.fori_loop(0, rows // 8, advance, start)
    for tile in range(tiles):
        at = slice(tile * LANES, (tile + 1) * LANES)
        y = y_s[pl.ds(tile, rows, stride=tiles), :]
        z = z_ref[:, at].astype(jnp.float32)
        y = y + skip_ref[:, at] * x_ref[:, at].astype(jnp.float32)
        o_ref[:, at] = (y * (z / (1.0 + jnp.exp(-z)))).astype(o_ref.dtype)


def scan_layer(cols, dt_proj, dt_bias, mamba_x, gate_z, decay_rate, skip_gain, start_state):
    rows, width = mamba_x.shape
    tiles = width // LANES
    rate = (decay_rate * (-LOG2E)).reshape(STATE, tiles, LANES)
    start = start_state.astype(jnp.float32).reshape(STATE, tiles, LANES)
    return pl.pallas_call(
        scan_kernel,
        out_shape=jax.ShapeDtypeStruct((rows, width), jnp.bfloat16),
        in_specs=[pl.BlockSpec(memory_space=pltpu.VMEM)] * 8,
        out_specs=pl.BlockSpec(memory_space=pltpu.VMEM),
        scratch_shapes=[
            pltpu.VMEM((rows * tiles, LANES), jnp.float32),
            pltpu.VMEM((rows * tiles, LANES), jnp.float32),
            pltpu.VMEM((rows * tiles, LANES), jnp.float32),
            pltpu.VMEM((2 * STATE, rows, LANES), jnp.float32),
        ],
        compiler_params=pltpu.CompilerParams(vmem_limit_bytes=56 * 2**20),
        cost_estimate=pl.CostEstimate(
            flops=30 * 10**9, bytes_accessed=10 * 2**20, transcendentals=rows * STATE * width
        ),
        name="scan_tokens",
    )(cols, dt_proj, dt_bias[None], mamba_x, gate_z, rate, skip_gain[None], start)


def body(
    queries,
    suffix_kv,
    page_pool,
    prefix_pages,
    prefix_len,
    mamba_x,
    gate_z,
    x_proj,
    dt_proj,
    dt_bias,
    decay_rate,
    skip_gain,
    state_pool,
    state_src,
):
    devices = lax.axis_size("req")
    cap = max(3, MAXPG // devices + 1)
    pool_dev = page_pool.shape[0]
    spool = state_pool.shape[0]
    places = page_places(prefix_pages[0], pool_dev, cap)
    wanted = pack_asks(prefix_pages[0], places, pool_dev, jnp.arange(devices * cap)).reshape(
        devices, cap
    )
    my_src = state_src[0]
    state_want = jnp.where(jnp.arange(devices) == my_src // spool, my_src % spool, -1)[:, None]
    asks = lax.all_to_all(
        jnp.concatenate([wanted, state_want], axis=1), "req", split_axis=0, concat_axis=0, tiled=True
    )
    partial_cols = jnp.dot(mamba_x, x_proj, preferred_element_type=jnp.float32)
    cols = lax.psum(partial_cols.astype(jnp.bfloat16), "tp")
    state_asks = asks[:, cap]
    state_send = state_pool[jnp.where(state_asks >= 0, state_asks, 0)]
    got_states = lax.all_to_all(state_send, "req", split_axis=0, concat_axis=0, tiled=True)
    sends = gather_pages(page_pool, asks[:, :cap].reshape(-1))
    got = [lax.all_to_all(send, "req", split_axis=0, concat_axis=0, tiled=True) for send in sends]
    start_state = lax.dynamic_index_in_dim(got_states, my_src // spool, 0, keepdims=False)
    mamba_out = scan_layer(
        cols, dt_proj, dt_bias, mamba_x, gate_z, decay_rate, skip_gain, start_state
    )
    attn_out = None
    for part, pages in enumerate(got):
        attn_out = attend(part, places, prefix_len, queries, suffix_kv, pages, attn_out)
    return (attn_out, mamba_out)


def solution(mesh):
    return jax.shard_map(
        body,
        mesh=mesh,
        in_specs=(
            P("req", "tp"),
            P(None, "req", "tp"),
            P("req", None, None, "tp"),
            P("req", None),
            P("req"),
            P("req", "tp"),
            P("req", "tp"),
            P("tp", None),
            P(None, "tp"),
            P("tp"),
            P(None, "tp"),
            P("tp"),
            P("req", None, "tp"),
            P("req"),
        ),
        out_specs=(P("req", "tp"), P("req", "tp")),
        check_vma=False,
    )
```

profile of v0, /device:TPU:4, one launch (start us, length us, event | category | flops | bytes accessed | tf_op | source)
XLA Modules:
  0.0 355.0 jit_solution(3797995284023656257)
XLA Ops:
  7.2 0.0 copy-start
  8.0 0.7 compare_select_fusion.9
  8.7 0.7 fusion.9
  9.3 0.2 convert_reduce_fusion
  9.5 0.7 fusion.5
  10.2 0.1 select_reduce_fusion
  10.3 0.1 sub.22
  10.4 0.1 pad_add_fusion
  10.4 11.1 %all_to_all.27 = s32[8,1,10]{2,1,0:T(1,128)S(1)} all-to-all(s32[8,1,10]{2,1,0:T(1,128)S(1)} %bitcast.48), channel_id=1, replica_groups=mesh['req'=8,'tp'=4] {'req'}, dimensions={0} | all-to-all | bytes 640 | tf_op jit(solution)/shard_map/all_to_all | solution.py:311
  21.6 0.2 fusion.1
  21.8 2.3 gather_fusion
  24.1 4.9 %all-to-all-start.3 = ((bf16[8,16,2048]{2,1,0:T(8,128)(2,1)}), bf16[8,16,2048]{2,1,0:T(8,128)(2,1)S(1)}, u32[]{:S(2)}, u32[]{:S(2)}) async-start(bf16[8,16,2048]{2,1,0:T(8,128)(2,1)} %gather_fusion), calls=%async_computation.3 | async-start | bytes 1048576 | tf_op jit(solution)/shard_map/all_to_all | solution.py:318
  29.0 0.6 reshape.65.asks
  29.5 144.7 %gather_pages.1 = (bf16[72,2,64,128]{3,2,1,0:T(8,128)(2,1)}, bf16[72,2,64,128]{3,2,1,0:T(8,128)(2,1)}) custom-call(s32[72]{0:T(128)} %reshape.65.asks, bf16[64,2,64,256]{3,2,1,0:T(8,128)(2,1)} %pool.1), custom_call_target="tpu_custom_call" | custom-call | tf_op jit(solution)/shard_map/gather_pages/pallas_call | solution.py:59
  174.3 0.0 all-to-all-done.3
  174.3 6.0 %all-to-all-start.2 = ((bf16[72,2,64,128]{3,2,1,0:T(8,128)(2,1)}), bf16[72,2,64,128]{3,2,1,0:T(8,128)(2,1)}, u32[]{:S(2)}, u32[]{:S(2)}) async-start(bf16[72,2,64,128]{3,2,1,0:T(8,128)(2,1)} %get-tuple-element.5), calls=%async_computation.2 | async-start | bytes 4718592 | tf_op jit(solution)/shard_map/all_to_all | solution.py:320
  180.3 0.0 copy-start.4
  180.3 0.0 all-reduce.2.cloned.1.call-start
  180.3 0.0 copy-done
  180.3 3.0 convolution_convert_fusion
  183.3 0.0 copy-start.5
  183.3 1.1 copy.24
  184.4 0.0 all-reduce.2.cloned.1.call-update
  185.1 0.0 copy-done.4
  185.1 0.7 copy.25
  185.8 0.0 copy-done.5
  185.9 0.7 copy.26
  186.5 45.5 %all-to-all-done.2.pages_ref = bf16[72,2,64,128]{3,2,1,0:T(8,128)(2,1)} async-done(((bf16[72,2,64,128]{3,2,1,0:T(8,128)(2,1)}), bf16[72,2,64,128]{3,2,1,0:T(8,128)(2,1)}, u32[]{:S(2)}, u32[]{:S(2)}) %all-to-all-start.2) | async-done | bytes 2359328 | tf_op jit(solution)/shard_map/all_to_all | solution.py:320
  232.0 4.8 %all-to-all-start.1 = ((bf16[72,2,64,128]{3,2,1,0:T(8,128)(2,1)}), bf16[72,2,64,128]{3,2,1,0:T(8,128)(2,1)}, u32[]{:S(2)}, u32[]{:S(2)}) async-start(bf16[72,2,64,128]{3,2,1,0:T(8,128)(2,1)} %get-tuple-element.4), calls=%async_computation.1 | async-start | bytes 4718592 | tf_op jit(solution)/shard_map/all_to_all | solution.py:320
  236.9 0.0 all-reduce.2.cloned.1.call-done.cols_ref
  236.9 0.0 copy-start.1
  236.9 0.0 copy-start.3
  236.9 31.6 %scan_tokens.1 = bf16[512,2048]{1,0:T(8,128)(2,1)} custom-call(bf16[512,544]{1,0:T(8,128)(2,1)} %all-reduce.2.cloned.1.call-done.cols_ref, bf16[512,2048]{1,0:T(8,128)(2,1)} %dtp_ref.1, f32[1,2048]{1,0:T(1,128)} %bitcast.49, bf16[512,2048]{1,0:T(8,128)(2,1)} %x_ref.1, bf16[512,2048]{1,0:T(8,128)(2,1)} %z_ref.1, f32[16,16,128]{2,1,0:T(8,128)} %bitcast.44, ...), custom_call_target="tpu_custom_call" | custom-call | flops 30000001024 | bytes 10485760 | tf_op jit(solution)/shard_map/scan_tokens/pallas_call | solution.py:266
  268.5 0.0 copy-done.1
  268.5 0.0 copy-done.3
  268.5 39.1 %attend_cached.2.rest_0_ = bf16[512,2048]{1,0:T(8,128)(2,1)} custom-call(s32[64]{0:T(128)S(1)} %compare_select_fusion.8.places, s32[1]{0:T(128)S(6)} %copy.29.plen_ref, bf16[512,2048]{1,0:T(8,128)(2,1)S(1)} %copy-done.1, bf16[2,512,256]{2,1,0:T(8,128)(2,1)S(1)} %copy-done.3, bf16[72,2,64,128]{3,2,1,0:T(8,128)(2,1)} %all-to-all-done.2.pages_ref), custom_call_target="tpu_custom_call" | custom-call | flops 19327352832 | bytes 8388608 | tf_op jit(solution)/shard_map/attend_cached/pallas_call | solution.py:175
  307.6 0.0 all-to-all-done.1.pages_ref
  307.6 0.0 copy-start.2
  307.6 1.6 copy-done.2
  309.2 38.9 %attend_cached.3 = bf16[512,2048]{1,0:T(8,128)(2,1)} custom-call(s32[64]{0:T(128)S(1)} %compare_select_fusion.8.places, s32[1]{0:T(128)S(6)} %copy.29.plen_ref, bf16[512,2048]{1,0:T(8,128)(2,1)S(1)} %copy-done.2, bf16[2,512,256]{2,1,0:T(8,128)(2,1)S(1)} %copy-done.3, ...), custom_call_target="tpu_custom_call", output_to_operand_aliasing={{}: (5, {})} | custom-call | flops 19327352832 | bytes 8388608 | tf_op jit(solution)/shard_map/attend_cached/pallas_call | solution.py:175
  (6 shorter events, 0.1 us)
Async XLA Ops:
  7.2 173.2 %copy-start = (bf16[2048,544]{0,1:T(8,128)(2,1)S(1)}, bf16[2048,544]{0,1:T(8,128)(2,1)}, u32[]{:S(2)}) copy-start(bf16[2048,544]{0,1:T(8,128)(2,1)} %param.21) | copy-start | bytes 6684676
  24.1 150.2 %all-to-all-start.3 = ((bf16[8,16,2048]{2,1,0:T(8,128)(2,1)}), bf16[8,16,2048]{2,1,0:T(8,128)(2,1)S(1)}, u32[]{:S(2)}, u32[]{:S(2)}) async-start(bf16[8,16,2048]{2,1,0:T(8,128)(2,1)} %gather_fusion), calls=%async_computation.3 | async-start | bytes 1048576 | tf_op jit(solution)/shard_map/all_to_all | solution.py:318
  174.3 57.7 %all-to-all-start.2 = ((bf16[72,2,64,128]{3,2,1,0:T(8,128)(2,1)}), bf16[72,2,64,128]{3,2,1,0:T(8,128)(2,1)}, u32[]{:S(2)}, u32[]{:S(2)}) async-start(bf16[72,2,64,128]{3,2,1,0:T(8,128)(2,1)} %get-tuple-element.5), calls=%async_computation.2 | async-start | bytes 4718592 | tf_op jit(solution)/shard_map/all_to_all | solution.py:320
  180.3 4.8 %copy-start.4 = (f32[16,2048]{1,0:T(8,128)S(1)}, f32[16,2048]{1,0:T(8,128)}, u32[]{:S(2)}) copy-start(f32[16,2048]{1,0:T(8,128)} %param.24) | copy-start | bytes 393220
  180.3 56.5 %all-reduce.2.cloned.1.call-start = ((), (), s32[]{:S(2)}) async-start(), calls=%async_computation.4 | async-start | bytes 1310720 | tf_op jit(solution)/shard_map/psum | solution.py:315
  183.3 2.5 copy-start.5
  232.0 75.6 %all-to-all-start.1 = ((bf16[72,2,64,128]{3,2,1,0:T(8,128)(2,1)}), bf16[72,2,64,128]{3,2,1,0:T(8,128)(2,1)}, u32[]{:S(2)}, u32[]{:S(2)}) async-start(bf16[72,2,64,128]{3,2,1,0:T(8,128)(2,1)} %get-tuple-element.4), calls=%async_computation.1 | async-start | bytes 4718592 | tf_op jit(solution)/shard_map/all_to_all | solution.py:320
  236.9 31.6 %copy-start.1 = (bf16[512,2048]{1,0:T(8,128)(2,1)S(1)}, bf16[512,2048]{1,0:T(8,128)(2,1)}, u32[]{:S(2)}) copy-start(bf16[512,2048]{1,0:T(8,128)(2,1)} %q_ref.3) | copy-start | bytes 6291460
  236.9 31.6 %copy-start.3 = (bf16[2,512,256]{2,1,0:T(8,128)(2,1)S(1)}, bf16[2,512,256]{2,1,0:T(8,128)(2,1)}, u32[]{:S(2)}) copy-start(bf16[2,512,256]{2,1,0:T(8,128)(2,1)} %kv_ref.3) | copy-start | bytes 1572868
  307.6 1.6 copy-start.2
Sparse Core Ops, SparseCore 0:
  184.6 34.7 all-reduce.1
where the time goes:
time: 356 us; the launch traced here: 355 us
  Pallas kernels  254 us (71%)
  waiting for transfers between devices  45.5 us (13%)
  starting transfers between devices  15.8 us (4%)
  between operations  15.6 us (4%)
  blocking collectives  11.1 us (3%)
  local copies, waits for them, and re-layouts  7.03 us (2%)
    pallas_call x1, Pallas kernels, gather_pages(): pl.pallas_call(functools.partial(gather_kernel, slots, parts), out_shape=...  145 us
    pallas_call x2, Pallas kernels, attend(): pl.pallas_call(attend_kernel, out_shape=jax.ShapeDtypeStruct((rows, width...  78.1 us
    all_to_all x2, waiting for transfers between devices, body(): lax.all_to_all(send, 'req', split_axis=0, concat_axis=0, tiled=True)  45.5 us
    pallas_call x1, Pallas kernels, scan_layer(): pl.pallas_call(scan_kernel, out_shape=jax.ShapeDtypeStruct((rows, width),...  31.6 us
    all_to_all x1, blocking collectives, body(): lax.all_to_all(jnp.concatenate([wanted, state_want], axis=1), 'req', spli...  11.1 us
    all_to_all x2, starting transfers between devices, body(): lax.all_to_all(send, 'req', split_axis=0, concat_axis=0, tiled=True)  10.9 us
  transfers between devices with their start and end apart: 4, of which 1 were waited for; matrix products, arithmetic and copies ran while one was open for 2% of the time, Pallas kernels for 61%

commit v1 on v0

--- a/solution.py
+++ b/solution.py
@@ -34,37 +34,39 @@
     return jnp.sum(jnp.where(hit, local[..., None, :] + 1, 0), axis=-1) - 1
 
 
-def gather_kernel(slots, parts, asks, pool, *rest):
-    outs, sem = rest[:parts], rest[parts]
+def gather_kernel(part, asks, pool, out, held, sem):
+    slots = held.shape[0]
 
     def start(slot, carry):
         page = jnp.maximum(asks[slot], 0)
-        for part in range(parts):
-            pltpu.make_async_copy(
-                pool.at[page, :, :, pl.ds(part * LANES, LANES)],
-                outs[part].at[slot],
-                sem.at[part],
-            ).start()
+        pltpu.make_async_copy(
+            pool.at[page, :, :, pl.ds(part * LANES, LANES)], held.at[slot], sem.at[0]
+        ).start()
         return carry
 
     lax.fori_loop(0, slots, start, 0)
-    for part in range(parts):
-        pltpu.make_async_copy(outs[part], outs[part], sem.at[part]).wait()
-
-
-def gather_pages(page_pool, asks):
-    slots = asks.shape[0]
-    parts = page_pool.shape[3] // LANES
-    one = jax.ShapeDtypeStruct((slots,) + page_pool.shape[1:3] + (LANES,), page_pool.dtype)
+    pltpu.make_async_copy(held, held, sem.at[0]).wait()
+    whole = pltpu.make_async_copy(held, out, sem.at[1])
+    whole.start()
+    whole.wait()
+
+
+def gather_pages(part, page_pool, asks):
+    shape = asks.shape + page_pool.shape[1:3] + (LANES,)
     return pl.pallas_call(
-        functools.partial(gather_kernel, slots, parts),
-        out_shape=(one,) * parts,
+        functools.partial(gather_kernel, part),
+        out_shape=jax.ShapeDtypeStruct(shape, page_pool.dtype),
         in_specs=[
             pl.BlockSpec(memory_space=pltpu.SMEM),
             pl.BlockSpec(memory_space=pl.ANY),
         ],
-        out_specs=(pl.BlockSpec(memory_space=pl.ANY),) * parts,
-        scratch_shapes=[pltpu.SemaphoreType.DMA((parts,))],
+        out_specs=pl.BlockSpec(memory_space=pl.ANY),
+        scratch_shapes=[
+            pltpu.VMEM(shape, page_pool.dtype),
+            pltpu.SemaphoreType.DMA((2,)),
+        ],
+        compiler_params=pltpu.CompilerParams(vmem_limit_bytes=48 * 2**20),
+        cost_estimate=pl.CostEstimate(flops=0, bytes_accessed=8 * 2**20, transcendentals=0),
         name="gather_pages",
     )(asks, page_pool)
 
@@ -308,22 +310,27 @@
     )
     my_src = state_src[0]
     state_want = jnp.where(jnp.arange(devices) == my_src // spool, my_src % spool, -1)[:, None]
-    asks = lax.all_to_all(
-        jnp.concatenate([wanted, state_want], axis=1), "req", split_axis=0, concat_axis=0, tiled=True
-    )
+    wanted = jnp.concatenate([wanted, state_want], axis=1)
     partial_cols = jnp.dot(mamba_x, x_proj, preferred_element_type=jnp.float32)
-    cols = lax.psum(partial_cols.astype(jnp.bfloat16), "tp")
+    partial_cols, wanted = lax.optimization_barrier((partial_cols.astype(jnp.bfloat16), wanted))
+    cols = lax.psum(partial_cols, "tp")
+    asks = lax.all_to_all(wanted, "req", split_axis=0, concat_axis=0, tiled=True)
+    page_asks = asks[:, :cap].reshape(-1)
     state_asks = asks[:, cap]
     state_send = state_pool[jnp.where(state_asks >= 0, state_asks, 0)]
     got_states = lax.all_to_all(state_send, "req", split_axis=0, concat_axis=0, tiled=True)
-    sends = gather_pages(page_pool, asks[:, :cap].reshape(-1))
-    got = [lax.all_to_all(send, "req", split_axis=0, concat_axis=0, tiled=True) for send in sends]
     start_state = lax.dynamic_index_in_dim(got_states, my_src // spool, 0, keepdims=False)
-    mamba_out = scan_layer(
-        cols, dt_proj, dt_bias, mamba_x, gate_z, decay_rate, skip_gain, start_state
-    )
-    attn_out = None
-    for part, pages in enumerate(got):
+    parts = page_pool.shape[3] // LANES
+    attn_out = mamba_out = None
+    for part in range(parts):
+        send = gather_pages(part, page_pool, page_asks)
+        if part == 1:
+            send, mamba_out = lax.optimization_barrier((send, mamba_out))
+        pages = lax.all_to_all(send, "req", split_axis=0, concat_axis=0, tiled=True)
+        if part == 0:
+            mamba_out = scan_layer(
+                cols, dt_proj, dt_bias, mamba_x, gate_z, decay_rate, skip_gain, start_state
+            )
         attn_out = attend(part, places, prefix_len, queries, suffix_kv, pages, attn_out)
     return (attn_out, mamba_out)
 

time: 356 us -> 230 us (0.65)
  Pallas kernels: 254 us -> 116 us
  waiting for transfers between devices: 45.5 us -> 52.4 us
    pallas_call x1 -> x2, Pallas kernels: 145 us -> 5.3 us  [gather_pages(): pl.pallas_call(functools.partial(gather_kernel, part), out_shape=jax.Shap...]
    all_to_all x2, waiting for transfers between devices: 45.5 us -> 10.7 us  [body(): pages = lax.all_to_all(send, 'req', split_axis=0, concat_axis=0, tiled=True)]
    psum x1, waiting for transfers between devices: 0.01 us -> 32.4 us  [body(): cols = lax.psum(partial_cols, 'tp')]
    all_to_all x1, waiting for transfers between devices: 0.01 us -> 8.61 us  [body(): lax.all_to_all(state_send, 'req', split_axis=0, concat_axis=0, tiled=True)]
    unnamed x14 -> x20, local copies, waits for them, and re-layouts: 2.97 us -> 7.38 us
  transfers between devices with their start and end apart: 4 -> 4, of which waited for: 1 -> 3; matrix products, arithmetic and copies ran while one was open for 2% -> 1% of each run, Pallas kernels for 61% -> 34%
where the time goes in v1:
time: 230 us; the launch traced here: 227 us
  Pallas kernels  116 us (50%)
  waiting for transfers between devices  52.4 us (23%)
  starting transfers between devices  15.9 us (7%)
  between operations  15.6 us (7%)
  blocking collectives  11.1 us (5%)
  local copies, waits for them, and re-layouts  8.91 us (4%)
  matrix products  4.31 us (2%)
  other arithmetic  2.6 us (1%)
    pallas_call x2, Pallas kernels, attend(): pl.pallas_call(attend_kernel, out_shape=jax.ShapeDtypeStruct((rows, width...  79 us
    psum x1, waiting for transfers between devices, body(): cols = lax.psum(partial_cols, 'tp')  32.4 us
    pallas_call x1, Pallas kernels, scan_layer(): pl.pallas_call(scan_kernel, out_shape=jax.ShapeDtypeStruct((rows, width),...  31.9 us
    all_to_all x1, blocking collectives, body(): lax.all_to_all(wanted, 'req', split_axis=0, concat_axis=0, tiled=True)  11.1 us
    all_to_all x2, starting transfers between devices, body(): pages = lax.all_to_all(send, 'req', split_axis=0, concat_axis=0, tiled=True)  11 us
    all_to_all x2, waiting for transfers between devices, body(): pages = lax.all_to_all(send, 'req', split_axis=0, concat_axis=0, tiled=True)  10.7 us
    all_to_all x1, waiting for transfers between devices, body(): lax.all_to_all(state_send, 'req', split_axis=0, concat_axis=0, tiled=True)  8.61 us
    unnamed x20, local copies, waits for them, and re-layouts  7.38 us
  transfers between devices with their start and end apart: 4, of which 3 were waited for; matrix products, arithmetic and copies ran while one was open for 1% of the time, Pallas kernels for 34%

profile of v1, /device:TPU:4, one launch (start us, length us, event | category | flops | bytes accessed | tf_op | source)
XLA Modules:
  0.0 227.1 jit_solution(1527016764820668502)
XLA Ops:
  7.2 0.0 copy-start
  8.0 0.7 compare_select_fusion.9
  8.7 0.7 fusion.9
  9.3 0.2 convert_reduce_fusion
  9.5 0.7 fusion.5
  10.2 0.1 select_reduce_fusion
  10.3 0.1 sub.22
  10.4 0.1 pad_add_fusion
  10.4 0.0 copy-done
  10.4 0.0 copy-start.6
  10.4 4.3 %convolution_convert_fusion = bf16[512,544]{1,0:T(8,128)(2,1)} fusion(bf16[512,2048]{1,0:T(8,128)(2,1)} %x_ref.1, bf16[2048,544]{0,1:T(8,128)(2,1)S(1)} %copy-done), kind=kOutput, calls=%fused_computation.1 | convolution fusion | flops 1141129216 | bytes 4882432 | tf_op jit(solution)/shard_map/dot_general | solution.py:314
  14.8 11.1 %all_to_all.27 = s32[8,1,10]{2,1,0:T(1,128)S(1)} all-to-all(s32[8,1,10]{2,1,0:T(1,128)S(1)} %bitcast.48), channel_id=1, replica_groups=mesh['req'=8,'tp'=4] {'req'}, dimensions={0} | all-to-all | bytes 640 | tf_op jit(solution)/shard_map/all_to_all | solution.py:317
  25.9 0.2 fusion.1
  26.1 0.0 copy-done.6
  26.1 1.4 gather_fusion
  27.5 4.9 %all-to-all-start.1 = ((bf16[8,16,2048]{2,1,0:T(8,128)(2,1)}), bf16[8,16,2048]{2,1,0:T(8,128)(2,1)S(1)}, u32[]{:S(2)}, u32[]{:S(2)}) async-start(bf16[8,16,2048]{2,1,0:T(8,128)(2,1)} %gather_fusion), calls=%async_computation.1 | async-start | bytes 1048576 | tf_op jit(solution)/shard_map/all_to_all | solution.py:321
  32.3 0.1 reshape.65.asks
  32.4 2.7 %gather_pages.3 = bf16[72,2,64,128]{3,2,1,0:T(8,128)(2,1)S(1)} custom-call(s32[72]{0:T(128)S(1)} %reshape.65.asks, bf16[64,2,64,256]{3,2,1,0:T(8,128)(2,1)} %pool.3), custom_call_target="tpu_custom_call" | custom-call | bytes 8388608 | tf_op jit(solution)/shard_map/gather_pages/pallas_call | solution.py:56
  35.1 0.0 copy-start.1
  35.1 1.4 copy-done.1
  36.5 0.0 copy-start.7
  36.5 8.6 %all-to-all-done.1 = bf16[8,16,2048]{2,1,0:T(8,128)(2,1)S(1)} async-done(((bf16[8,16,2048]{2,1,0:T(8,128)(2,1)}), bf16[8,16,2048]{2,1,0:T(8,128)(2,1)S(1)}, u32[]{:S(2)}, u32[]{:S(2)}) %all-to-all-start.1) | async-done | bytes 524320 | tf_op jit(solution)/shard_map/all_to_all | solution.py:321
  45.1 4.8 %all-to-all-start.3 = ((bf16[72,2,64,128]{3,2,1,0:T(8,128)(2,1)}), bf16[72,2,64,128]{3,2,1,0:T(8,128)(2,1)}, u32[]{:S(2)}, u32[]{:S(2)}) async-start(bf16[72,2,64,128]{3,2,1,0:T(8,128)(2,1)} %copy-done.1), calls=%async_computation.3 | async-start | bytes 4718592 | tf_op jit(solution)/shard_map/all_to_all | solution.py:329
  49.9 0.0 all-reduce.2.cloned.1.call-start
  49.9 0.7 all-reduce.2.cloned.1.call-update
  50.7 0.0 copy-done.7
  50.7 0.7 copy.24
  51.4 2.6 %gather_pages.2 = bf16[72,2,64,128]{3,2,1,0:T(8,128)(2,1)S(1)} custom-call(s32[72]{0:T(128)S(1)} %reshape.65.asks, bf16[64,2,64,256]{3,2,1,0:T(8,128)(2,1)} %pool.3), custom_call_target="tpu_custom_call" | custom-call | bytes 8388608 | tf_op jit(solution)/shard_map/gather_pages/pallas_call | solution.py:56
  54.0 0.0 copy-start.2
  54.0 1.4 copy-done.2
  55.4 0.7 copy.25
  56.1 32.4 %all-reduce.2.cloned.1.call-done.cols_ref = bf16[512,544]{1,0:T(8,128)(2,1)} async-done(((bf16[512,544]{1,0:T(8,128)(2,1)}), bf16[512,544]{1,0:T(8,128)(2,1)}) %all-reduce.2.cloned.1.call-update) | async-done | bytes 557072 | tf_op jit(solution)/shard_map/psum | solution.py:316
  88.5 31.9 %scan_tokens.1 = bf16[512,2048]{1,0:T(8,128)(2,1)} custom-call(bf16[512,544]{1,0:T(8,128)(2,1)} %all-reduce.2.cloned.1.call-done.cols_ref, bf16[512,2048]{1,0:T(8,128)(2,1)} %dtp_ref.1, f32[1,2048]{1,0:T(1,128)} %bitcast.49, bf16[512,2048]{1,0:T(8,128)(2,1)} %x_ref.1, bf16[512,2048]{1,0:T(8,128)(2,1)} %z_ref.1, f32[16,16,128]{2,1,0:T(8,128)} %bitcast.44, ...), custom_call_target="tpu_custom_call" | custom-call | flops 30000001024 | bytes 10485760 | tf_op jit(solution)/shard_map/scan_tokens/pallas_call | solution.py:268
  120.4 0.0 copy-start.8
  120.4 0.0 copy-start.5
  120.4 0.0 all-to-all-done.3.pages_ref
  120.4 6.2 %all-to-all-start.2 = ((bf16[72,2,64,128]{3,2,1,0:T(8,128)(2,1)}), bf16[72,2,64,128]{3,2,1,0:T(8,128)(2,1)}, u32[]{:S(2)}, u32[]{:S(2)}) async-start(bf16[72,2,64,128]{3,2,1,0:T(8,128)(2,1)} %copy-done.2), calls=%async_computation.2 | async-start | bytes 4718592 | tf_op jit(solution)/shard_map/all_to_all | solution.py:329
  127.3 0.0 copy-done.8
  127.3 0.0 copy-done.5
  127.3 0.0 copy-start.3
  127.3 1.6 copy-done.3
  128.9 39.5 %attend_cached.2.rest_0_ = bf16[512,2048]{1,0:T(8,128)(2,1)} custom-call(s32[64]{0:T(128)S(1)} %compare_select_fusion.8.places, s32[1]{0:T(128)S(6)} %copy.28.plen_ref, bf16[512,2048]{1,0:T(8,128)(2,1)S(1)} %copy-done.3, bf16[2,512,256]{2,1,0:T(8,128)(2,1)S(1)} %copy-done.5, bf16[72,2,64,128]{3,2,1,0:T(8,128)(2,1)} %all-to-all-done.3.pages_ref), custom_call_target="tpu_custom_call" | custom-call | flops 19327352832 | bytes 8388608 | tf_op jit(solution)/shard_map/attend_cached/pallas_call | solution.py:177
  168.4 10.7 %all-to-all-done.2.pages_ref = bf16[72,2,64,128]{3,2,1,0:T(8,128)(2,1)} async-done(((bf16[72,2,64,128]{3,2,1,0:T(8,128)(2,1)}), bf16[72,2,64,128]{3,2,1,0:T(8,128)(2,1)}, u32[]{:S(2)}, u32[]{:S(2)}) %all-to-all-start.2) | async-done | bytes 2359328 | tf_op jit(solution)/shard_map/all_to_all | solution.py:329
  179.1 0.0 copy-start.4
  179.1 1.6 copy-done.4
  180.7 39.5 %attend_cached.3 = bf16[512,2048]{1,0:T(8,128)(2,1)} custom-call(s32[64]{0:T(128)S(1)} %compare_select_fusion.8.places, s32[1]{0:T(128)S(6)} %copy.28.plen_ref, bf16[512,2048]{1,0:T(8,128)(2,1)S(1)} %copy-done.4, bf16[2,512,256]{2,1,0:T(8,128)(2,1)S(1)} %copy-done.5, ...), custom_call_target="tpu_custom_call", output_to_operand_aliasing={{}: (5, {})} | custom-call | flops 19327352832 | bytes 8388608 | tf_op jit(solution)/shard_map/attend_cached/pallas_call | solution.py:177
  (6 shorter events, 0.1 us)
Async XLA Ops:
  7.2 3.3 %copy-start = (bf16[2048,544]{0,1:T(8,128)(2,1)S(1)}, bf16[2048,544]{0,1:T(8,128)(2,1)}, u32[]{:S(2)}) copy-start(bf16[2048,544]{0,1:T(8,128)(2,1)} %param.21) | copy-start | bytes 6684676
  10.4 15.6 %copy-start.6 = (bf16[4,16,2048]{2,1,0:T(8,128)(2,1)S(1)}, bf16[4,16,2048]{2,1,0:T(8,128)(2,1)}, u32[]{:S(2)}) copy-start(bf16[4,16,2048]{2,1,0:T(8,128)(2,1)} %param.26) | copy-start | bytes 786436
  27.5 17.7 %all-to-all-start.1 = ((bf16[8,16,2048]{2,1,0:T(8,128)(2,1)}), bf16[8,16,2048]{2,1,0:T(8,128)(2,1)S(1)}, u32[]{:S(2)}, u32[]{:S(2)}) async-start(bf16[8,16,2048]{2,1,0:T(8,128)(2,1)} %gather_fusion), calls=%async_computation.1 | async-start | bytes 1048576 | tf_op jit(solution)/shard_map/all_to_all | solution.py:321
  35.1 1.4 copy-start.1
  36.5 14.1 %copy-start.7 = (f32[16,2048]{1,0:T(8,128)S(1)}, f32[16,2048]{1,0:T(8,128)}, u32[]{:S(2)}) copy-start(f32[16,2048]{1,0:T(8,128)} %param.24) | copy-start | bytes 393220
  45.1 75.3 %all-to-all-start.3 = ((bf16[72,2,64,128]{3,2,1,0:T(8,128)(2,1)}), bf16[72,2,64,128]{3,2,1,0:T(8,128)(2,1)}, u32[]{:S(2)}, u32[]{:S(2)}) async-start(bf16[72,2,64,128]{3,2,1,0:T(8,128)(2,1)} %copy-done.1), calls=%async_computation.3 | async-start | bytes 4718592 | tf_op jit(solution)/shard_map/all_to_all | solution.py:329
  49.9 38.6 %all-reduce.2.cloned.1.call-start = ((), (), s32[]{:S(2)}) async-start(), calls=%async_computation.4 | async-start | bytes 1310720 | tf_op jit(solution)/shard_map/psum | solution.py:316
  54.0 1.4 copy-start.2
  120.4 6.9 %copy-start.8 = (s32[1,64]{1,0:T(1,128)S(1)}, s32[1,64]{1,0:T(1,128)}, u32[]{:S(2)}) copy-start(s32[1,64]{1,0:T(1,128)} %param.17) | copy-start | bytes 772
  120.4 6.9 %copy-start.5 = (bf16[2,512,256]{2,1,0:T(8,128)(2,1)S(1)}, bf16[2,512,256]{2,1,0:T(8,128)(2,1)}, u32[]{:S(2)}) copy-start(bf16[2,512,256]{2,1,0:T(8,128)(2,1)} %kv_ref.3) | copy-start | bytes 1572868
  120.4 58.7 %all-to-all-start.2 = ((bf16[72,2,64,128]{3,2,1,0:T(8,128)(2,1)}), bf16[72,2,64,128]{3,2,1,0:T(8,128)(2,1)}, u32[]{:S(2)}, u32[]{:S(2)}) async-start(bf16[72,2,64,128]{3,2,1,0:T(8,128)(2,1)} %copy-done.2), calls=%async_computation.2 | async-start | bytes 4718592 | tf_op jit(solution)/shard_map/all_to_all | solution.py:329
  127.3 1.6 copy-start.3
  179.1 1.6 copy-start.4
Sparse Core Ops, SparseCore 0:
  53.7 34.7 all-reduce.1

commit v2 on v1

--- a/solution.py
+++ b/solution.py
@@ -324,6 +324,8 @@
     attn_out = mamba_out = None
     for part in range(parts):
         send = gather_pages(part, page_pool, page_asks)
+        if part == 0:
+            send, cols = lax.optimization_barrier((send, cols))
         if part == 1:
             send, mamba_out = lax.optimization_barrier((send, mamba_out))
         pages = lax.all_to_all(send, "req", split_axis=0, concat_axis=0, tiled=True)

time: 230 us -> 236 us (1.026)
  waiting for transfers between devices: 52.4 us -> 59.5 us
    all_to_all x2, waiting for transfers between devices: 10.7 us -> 25.9 us  [body(): pages = lax.all_to_all(send, 'req', split_axis=0, concat_axis=0, tiled=True)]
    all_to_all x1, waiting for transfers between devices: 8.61 us -> 0.01 us  [body(): lax.all_to_all(state_send, 'req', split_axis=0, concat_axis=0, tiled=True)]
  transfers between devices with their start and end apart: 4 -> 4, of which waited for: 3 -> 3; matrix products, arithmetic and copies ran while one was open for 1% -> 1% of each run, Pallas kernels for 34% -> 33%
where the time goes in v2:
time: 236 us; the launch traced here: 235 us
  Pallas kernels  117 us (50%)
  waiting for transfers between devices  59.5 us (25%)
  starting transfers between devices  15.8 us (7%)
  between operations  15.6 us (7%)
  blocking collectives  11.1 us (5%)
  local copies, waits for them, and re-layouts  8.91 us (4%)
  matrix products  4.31 us (2%)
  other arithmetic  2.6 us (1%)
    pallas_call x2, Pallas kernels, attend(): pl.pallas_call(attend_kernel, out_shape=jax.ShapeDtypeStruct((rows, width...  79 us
    psum x1, waiting for transfers between devices, body(): cols = lax.psum(partial_cols, 'tp')  32.9 us
    pallas_call x1, Pallas kernels, scan_layer(): pl.pallas_call(scan_kernel, out_shape=jax.ShapeDtypeStruct((rows, width),...  31.9 us
    all_to_all x2, waiting for transfers between devices, body(): pages = lax.all_to_all(send, 'req', split_axis=0, concat_axis=0, tiled=True)  25.9 us
    all_to_all x1, blocking collectives, body(): lax.all_to_all(wanted, 'req', split_axis=0, concat_axis=0, tiled=True)  11.1 us
    all_to_all x2, starting transfers between devices, body(): pages = lax.all_to_all(send, 'req', split_axis=0, concat_axis=0, tiled=True)  10.9 us
    unnamed x20, local copies, waits for them, and re-layouts  7.38 us
    pallas_call x2, Pallas kernels, gather_pages(): pl.pallas_call(functools.partial(gather_kernel, part), out_shape=jax.Shap...  6.42 us
  transfers between devices with their start and end apart: 4, of which 3 were waited for; matrix products, arithmetic and copies ran while one was open for 1% of the time, Pallas kernels for 33%

profile of v2, /device:TPU:4, one launch (start us, length us, event | category | flops | bytes accessed | tf_op | source)
XLA Modules:
  0.0 235.1 jit_solution(12209501054714636651)
XLA Ops:
  7.2 0.0 copy-start
  8.0 0.7 compare_select_fusion.9
  8.7 0.7 fusion.9
  9.3 0.2 convert_reduce_fusion
  9.5 0.7 fusion.5
  10.2 0.1 select_reduce_fusion
  10.3 0.1 sub.22
  10.4 0.1 pad_add_fusion
  10.4 0.0 copy-done
  10.4 0.0 copy-start.6
  10.4 4.3 %convolution_convert_fusion = bf16[512,544]{1,0:T(8,128)(2,1)} fusion(bf16[512,2048]{1,0:T(8,128)(2,1)} %x_ref.1, bf16[2048,544]{0,1:T(8,128)(2,1)S(1)} %copy-done), kind=kOutput, calls=%fused_computation.1 | convolution fusion | flops 1141129216 | bytes 4882432 | tf_op jit(solution)/shard_map/dot_general | solution.py:314
  14.8 11.1 %all_to_all.27 = s32[8,1,10]{2,1,0:T(1,128)S(1)} all-to-all(s32[8,1,10]{2,1,0:T(1,128)S(1)} %bitcast.48), channel_id=1, replica_groups=mesh['req'=8,'tp'=4] {'req'}, dimensions={0} | all-to-all | bytes 640 | tf_op jit(solution)/shard_map/all_to_all | solution.py:317
  25.9 0.2 fusion.1
  26.1 0.0 copy-done.6
  26.1 1.4 gather_fusion
  27.5 4.9 %all-to-all-start.1 = ((bf16[8,16,2048]{2,1,0:T(8,128)(2,1)}), bf16[8,16,2048]{2,1,0:T(8,128)(2,1)S(1)}, u32[]{:S(2)}, u32[]{:S(2)}) async-start(bf16[8,16,2048]{2,1,0:T(8,128)(2,1)} %gather_fusion), calls=%async_computation.1 | async-start | bytes 1048576 | tf_op jit(solution)/shard_map/all_to_all | solution.py:321
  32.3 0.0 all-reduce.2.cloned.1.call-start
  32.3 0.7 all-reduce.2.cloned.1.call-update
  33.0 0.1 reshape.65.asks
  33.1 3.3 %gather_pages.3 = bf16[72,2,64,128]{3,2,1,0:T(8,128)(2,1)S(1)} custom-call(s32[72]{0:T(128)S(1)} %reshape.65.asks, bf16[64,2,64,256]{3,2,1,0:T(8,128)(2,1)} %pool.3), custom_call_target="tpu_custom_call" | custom-call | bytes 8388608 | tf_op jit(solution)/shard_map/gather_pages/pallas_call | solution.py:56
  36.4 0.0 copy-start.1
  36.4 1.4 copy-done.1
  37.9 0.0 copy-start.7
  37.9 32.9 %all-reduce.2.cloned.1.call-done.cols_ref = bf16[512,544]{1,0:T(8,128)(2,1)} async-done(((bf16[512,544]{1,0:T(8,128)(2,1)}), bf16[512,544]{1,0:T(8,128)(2,1)}) %all-reduce.2.cloned.1.call-update) | async-done | bytes 557072 | tf_op jit(solution)/shard_map/psum | solution.py:316
  70.8 0.0 all-to-all-done.1
  70.8 6.1 %all-to-all-start.3 = ((bf16[72,2,64,128]{3,2,1,0:T(8,128)(2,1)}), bf16[72,2,64,128]{3,2,1,0:T(8,128)(2,1)}, u32[]{:S(2)}, u32[]{:S(2)}) async-start(bf16[72,2,64,128]{3,2,1,0:T(8,128)(2,1)} %copy-done.1), calls=%async_computation.3 | async-start | bytes 4718592 | tf_op jit(solution)/shard_map/all_to_all | solution.py:331
  76.9 0.0 copy-done.7
  76.9 0.7 copy.24
  77.6 3.1 %gather_pages.2 = bf16[72,2,64,128]{3,2,1,0:T(8,128)(2,1)S(1)} custom-call(s32[72]{0:T(128)S(1)} %reshape.65.asks, bf16[64,2,64,256]{3,2,1,0:T(8,128)(2,1)} %pool.3), custom_call_target="tpu_custom_call" | custom-call | bytes 8388608 | tf_op jit(solution)/shard_map/gather_pages/pallas_call | solution.py:56
  80.7 0.0 copy-start.2
  80.7 1.4 copy-done.2
  82.1 0.7 copy.25
  82.8 31.9 %scan_tokens.1 = bf16[512,2048]{1,0:T(8,128)(2,1)} custom-call(bf16[512,544]{1,0:T(8,128)(2,1)} %all-reduce.2.cloned.1.call-done.cols_ref, bf16[512,2048]{1,0:T(8,128)(2,1)} %dtp_ref.1, f32[1,2048]{1,0:T(1,128)} %bitcast.49, bf16[512,2048]{1,0:T(8,128)(2,1)} %x_ref.1, bf16[512,2048]{1,0:T(8,128)(2,1)} %z_ref.1, f32[16,16,128]{2,1,0:T(8,128)} %bitcast.44, ...), custom_call_target="tpu_custom_call" | custom-call | flops 30000001024 | bytes 10485760 | tf_op jit(solution)/shard_map/scan_tokens/pallas_call | solution.py:268
  114.7 0.0 copy-start.8
  114.7 0.0 copy-start.5
  114.7 14.7 %all-to-all-done.3.pages_ref = bf16[72,2,64,128]{3,2,1,0:T(8,128)(2,1)} async-done(((bf16[72,2,64,128]{3,2,1,0:T(8,128)(2,1)}), bf16[72,2,64,128]{3,2,1,0:T(8,128)(2,1)}, u32[]{:S(2)}, u32[]{:S(2)}) %all-to-all-start.3) | async-done | bytes 2359328 | tf_op jit(solution)/shard_map/all_to_all | solution.py:331
  129.4 4.8 %all-to-all-start.2 = ((bf16[72,2,64,128]{3,2,1,0:T(8,128)(2,1)}), bf16[72,2,64,128]{3,2,1,0:T(8,128)(2,1)}, u32[]{:S(2)}, u32[]{:S(2)}) async-start(bf16[72,2,64,128]{3,2,1,0:T(8,128)(2,1)} %copy-done.2), calls=%async_computation.2 | async-start | bytes 4718592 | tf_op jit(solution)/shard_map/all_to_all | solution.py:331
  134.8 0.0 copy-done.8
  134.9 0.0 copy-done.5
  134.9 0.0 copy-start.3
  134.9 1.6 copy-done.3
  136.5 39.5 %attend_cached.2.rest_0_ = bf16[512,2048]{1,0:T(8,128)(2,1)} custom-call(s32[64]{0:T(128)S(1)} %compare_select_fusion.8.places, s32[1]{0:T(128)S(6)} %copy.28.plen_ref, bf16[512,2048]{1,0:T(8,128)(2,1)S(1)} %copy-done.3, bf16[2,512,256]{2,1,0:T(8,128)(2,1)S(1)} %copy-done.5, bf16[72,2,64,128]{3,2,1,0:T(8,128)(2,1)} %all-to-all-done.3.pages_ref), custom_call_target="tpu_custom_call" | custom-call | flops 19327352832 | bytes 8388608 | tf_op jit(solution)/shard_map/attend_cached/pallas_call | solution.py:177
  176.0 11.2 %all-to-all-done.2.pages_ref = bf16[72,2,64,128]{3,2,1,0:T(8,128)(2,1)} async-done(((bf16[72,2,64,128]{3,2,1,0:T(8,128)(2,1)}), bf16[72,2,64,128]{3,2,1,0:T(8,128)(2,1)}, u32[]{:S(2)}, u32[]{:S(2)}) %all-to-all-start.2) | async-done | bytes 2359328 | tf_op jit(solution)/shard_map/all_to_all | solution.py:331
  187.1 0.0 copy-start.4
  187.1 1.6 copy-done.4
  188.7 39.5 %attend_cached.3 = bf16[512,2048]{1,0:T(8,128)(2,1)} custom-call(s32[64]{0:T(128)S(1)} %compare_select_fusion.8.places, s32[1]{0:T(128)S(6)} %copy.28.plen_ref, bf16[512,2048]{1,0:T(8,128)(2,1)S(1)} %copy-done.4, bf16[2,512,256]{2,1,0:T(8,128)(2,1)S(1)} %copy-done.5, ...), custom_call_target="tpu_custom_call", output_to_operand_aliasing={{}: (5, {})} | custom-call | flops 19327352832 | bytes 8388608 | tf_op jit(solution)/shard_map/attend_cached/pallas_call | solution.py:177
  (6 shorter events, 0.1 us)
Async XLA Ops:
  7.2 3.3 %copy-start = (bf16[2048,544]{0,1:T(8,128)(2,1)S(1)}, bf16[2048,544]{0,1:T(8,128)(2,1)}, u32[]{:S(2)}) copy-start(bf16[2048,544]{0,1:T(8,128)(2,1)} %param.21) | copy-start | bytes 6684676
  10.4 15.6 %copy-start.6 = (bf16[4,16,2048]{2,1,0:T(8,128)(2,1)S(1)}, bf16[4,16,2048]{2,1,0:T(8,128)(2,1)}, u32[]{:S(2)}) copy-start(bf16[4,16,2048]{2,1,0:T(8,128)(2,1)} %param.26) | copy-start | bytes 786436
  27.5 43.3 %all-to-all-start.1 = ((bf16[8,16,2048]{2,1,0:T(8,128)(2,1)}), bf16[8,16,2048]{2,1,0:T(8,128)(2,1)S(1)}, u32[]{:S(2)}, u32[]{:S(2)}) async-start(bf16[8,16,2048]{2,1,0:T(8,128)(2,1)} %gather_fusion), calls=%async_computation.1 | async-start | bytes 1048576 | tf_op jit(solution)/shard_map/all_to_all | solution.py:321
  32.3 38.5 %all-reduce.2.cloned.1.call-start = ((), (), s32[]{:S(2)}) async-start(), calls=%async_computation.4 | async-start | bytes 1310720 | tf_op jit(solution)/shard_map/psum | solution.py:316
  36.4 1.4 copy-start.1
  37.9 39.0 %copy-start.7 = (f32[16,2048]{1,0:T(8,128)S(1)}, f32[16,2048]{1,0:T(8,128)}, u32[]{:S(2)}) copy-start(f32[16,2048]{1,0:T(8,128)} %param.24) | copy-start | bytes 393220
  70.8 58.6 %all-to-all-start.3 = ((bf16[72,2,64,128]{3,2,1,0:T(8,128)(2,1)}), bf16[72,2,64,128]{3,2,1,0:T(8,128)(2,1)}, u32[]{:S(2)}, u32[]{:S(2)}) async-start(bf16[72,2,64,128]{3,2,1,0:T(8,128)(2,1)} %copy-done.1), calls=%async_computation.3 | async-start | bytes 4718592 | tf_op jit(solution)/shard_map/all_to_all | solution.py:331
  80.7 1.4 copy-start.2
  114.7 20.2 %copy-start.8 = (s32[1,64]{1,0:T(1,128)S(1)}, s32[1,64]{1,0:T(1,128)}, u32[]{:S(2)}) copy-start(s32[1,64]{1,0:T(1,128)} %param.17) | copy-start | bytes 772
  114.7 20.2 %copy-start.5 = (bf16[2,512,256]{2,1,0:T(8,128)(2,1)S(1)}, bf16[2,512,256]{2,1,0:T(8,128)(2,1)}, u32[]{:S(2)}) copy-start(bf16[2,512,256]{2,1,0:T(8,128)(2,1)} %kv_ref.3) | copy-start | bytes 1572868
  129.4 57.8 %all-to-all-start.2 = ((bf16[72,2,64,128]{3,2,1,0:T(8,128)(2,1)}), bf16[72,2,64,128]{3,2,1,0:T(8,128)(2,1)}, u32[]{:S(2)}, u32[]{:S(2)}) async-start(bf16[72,2,64,128]{3,2,1,0:T(8,128)(2,1)} %copy-done.2), calls=%async_computation.2 | async-start | bytes 4718592 | tf_op jit(solution)/shard_map/all_to_all | solution.py:331
  134.9 1.6 copy-start.3
  187.1 1.6 copy-start.4
Sparse Core Ops, SparseCore 0:
  36.1 34.6 all-reduce.1
